TPU v7x, 32 devices: a whole 2x2x4 slice. The times are simulated.
32 devices in a mesh: grp: 4 (over y, x), col: 8 (over z, core).
Axes of the slice: x: 2, y: 2, z: 4, core: 2. Of those that a mesh axis runs over, the one named last changes fastest.
Arguments:
- inputs: bfloat16 [24, 256, 8192], P('grp', 'col'), may hold values from -6 to 6
- out_grads: bfloat16 [24, 256, 8192], P('grp', None, 'col'), may hold values from -0.5 to 0.5
- first_moment: float32 [8192, 8192], P(None, 'col'), may hold values from -2 to 2
- second_moment: float32 [8192, 8192], P(None, 'col'), may hold values from 0.01 to 1
- signs_in: int32 [8192], replicated, may hold values from 0 to 1
- signs_out: int32 [8192], replicated, may hold values from 0 to 1
- rows_in: int32 [64], replicated, may hold values from 0 to 8191, as said below
- rows_out: int32 [128], replicated, may hold values from 0 to 8191, as said below
- task_ids: int32 [24], P('grp'), may hold values from 0 to 7
- weights: int32 [24], P('grp'), may hold values from 1 to 4
Outputs:
- prototypes: float32 [8, 64, 128], P('grp', 'col')
Inputs may be any that keep to these rules, and one draw needn't show every extreme that they name: `rows_in`: distinct row numbers. `rows_out`: distinct row numbers.
All inputs are finite; a program needn't handle non-finite values.
Results may differ from a plain program's by a relative error of at most 0.0019.
Values may be sent and summed in bfloat16 or wider, within the bound.
No kernel may reach another device: no remote copies, remote signals or barrier semaphores. Data moves between devices by JAX's collectives and lax.ppermute only.
A program may use at most 256 MiB of HBM per device.

v0:
```python
import functools

import jax
import jax.numpy as jnp
from jax import lax
from jax.experimental import pallas as pl
from jax.experimental.pallas import tpu as pltpu
from jax.sharding import PartitionSpec as P

PRO_GRP = 2
CORES = 2
BLOCK = 512
TILE = 256


def signed_hadamard(rows, cols, sign_bits):
    parity = lax.population_count(jnp.bitwise_and(rows, cols)) + sign_bits
    return (1 - 2 * jnp.bitwise_and(parity, 1)).astype(jnp.bfloat16)


def sketch_kernel(n_parts, per, slots_ref, *refs):
    parts = refs[:n_parts]
    og_ref, first_ref, second_ref, left_ref, right_ref, out_ref = refs[n_parts : n_parts + 6]
    first_s, second_s, x_s, xt_0, xt_1, g_0, g_1, u_0, u_1, t_0, t_1 = refs[n_parts + 6 :]
    xt_s, g_s, u_s, t_s = (xt_0, xt_1), (g_0, g_1), (u_0, u_1), (t_0, t_1)
    examples, _, cols = og_ref.shape
    n_right = right_ref.shape[1]
    tile = g_0.shape[1]

    @pl.when(pl.program_id(0) == 0)
    def _():
        out_ref[...] = jnp.zeros_like(out_ref)

    first_s[...] = 9.0 * first_ref[...]
    second_s[...] = 99.9 * second_ref[...]
    items = [(e, c) for e in range(examples) for c in range(0, cols, tile)]

    if n_parts > 1:
        own_ref, sibling_ref = parts[:2]
        n_chunks = (n_parts - 2) // 2
        share = own_ref.shape[1]
        others = parts[2].shape[0]

        def place(slot, value):
            token = pl.multiple_of(slots_ref[slot] * share, share)
            x_s[:, pl.ds(token, share), :] = value

        place(0, own_ref[...])
        place(others + 1, sibling_ref[...])
        for k in range(n_chunks):

            @pl.when(pl.program_id(0) // per == k)
            def _():
                for j in range(others):
                    place(1 + j, parts[2 + k][j])
                    place(others + 2 + j, parts[2 + n_chunks + k][j])

    def load(e):
        xt_s[e % 2][...] = (parts[0][e] if n_parts == 1 else x_s[e]).T

    def make_grad(i):
        e, c = items[i]
        if c == 0:
            load(e)
        g_s[i % 2][...] = jnp.dot(
            xt_s[e % 2][...], og_ref[e, :, c : c + tile], preferred_element_type=jnp.float32
        )

    def make_update(i):
        e, c = items[i]
        g = g_s[i % 2][...]
        first = first_s[:, c : c + tile] + g
        second = second_s[:, c : c + tile] + (0.1 * g) * g
        bottom = second * lax.rsqrt(second) + 1e-07
        u_s[e % 2][:, c : c + tile] = (first * pl.reciprocal(bottom, approx=True)).astype(
            jnp.bfloat16
        )

    def times_right(i):
        e, c = items[i]
        t = jnp.dot(
            u_s[e % 2][:, c : c + tile],
            right_ref[c : c + tile, :],
            preferred_element_type=jnp.float32,
        )
        if c == 0:
            t_s[e % 2][...] = t
        else:
            t_s[e % 2][...] += t

    def times_left(i):
        e, c = items[i]
        if c + tile != cols:
            return
        t = t_s[e % 2][...]
        high = t.astype(jnp.bfloat16)
        low = (t - high.astype(jnp.float32)).astype(jnp.bfloat16)
        both = jnp.dot(
            left_ref[...],
            jnp.concatenate([high, low], axis=1),
            preferred_element_type=jnp.float32,
        )
        out_ref[e] += both[:, :n_right] + both[:, n_right:]

    stages = (make_grad, make_update, times_right, times_left)
    for step in range(len(items) + len(stages) - 1):
        for lag, stage in enumerate(stages):
            if 0 <= step - lag < len(items):
                stage(step - lag)


def piece_sketch(slots, parts, out_grads, first, second, left, right, start, rows):
    examples, tokens, cols = out_grads.shape
    n_left, n_right = left.shape[0], right.shape[1]
    block = min(BLOCK, rows)
    tile = min(TILE, cols)
    at = start // block

    n_chunks = (len(parts) - 2) // 2
    per = rows // block // n_chunks if n_chunks > 0 else 1

    def part_spec(i, part):
        if part.ndim == 3:
            return pl.BlockSpec(part.shape[:2] + (block,), lambda i: (0, 0, i))
        first_block = (i - 2) % n_chunks * per
        return pl.BlockSpec(
            part.shape[:3] + (block,),
            lambda i: (0, 0, 0, jnp.clip(i - first_block, 0, per - 1)),
        )

    return pl.pallas_call(
        functools.partial(sketch_kernel, len(parts), per),
        grid=(rows // block,),
        in_specs=[pl.BlockSpec(memory_space=pltpu.SMEM)]
        + [part_spec(i, part) for i, part in enumerate(parts)]
        + [
            pl.BlockSpec((examples, tokens, cols), lambda i: (0, 0, 0)),
            pl.BlockSpec((block, cols), lambda i: (i + at, 0)),
            pl.BlockSpec((block, cols), lambda i: (i + at, 0)),
            pl.BlockSpec((n_left, block), lambda i: (0, i + at)),
            pl.BlockSpec((cols, n_right), lambda i: (0, 0)),
        ],
        out_specs=pl.BlockSpec((examples, n_left, n_right), lambda i: (0, 0, 0)),
        out_shape=jax.ShapeDtypeStruct((examples, n_left, n_right), jnp.float32),
        scratch_shapes=[pltpu.VMEM((block, cols), jnp.float32)] * 2
        + [pltpu.VMEM((examples, tokens, block) if n_chunks > 0 else (1, 16, 128), jnp.bfloat16)]
        + [pltpu.VMEM((block, tokens), jnp.bfloat16)] * 2
        + [pltpu.VMEM((block, tile), jnp.float32)] * 2
        + [pltpu.VMEM((block, cols), jnp.bfloat16)] * 2
        + [pltpu.VMEM((block, n_right), jnp.float32)] * 2,
        compiler_params=pltpu.CompilerParams(
            vmem_limit_bytes=48 * 1024 * 1024, dimension_semantics=("arbitrary",)
        ),
        cost_estimate=pl.CostEstimate(flops=1, bytes_accessed=1, transcendentals=0),
        name="piece_sketch",
    )(slots, *parts, out_grads, first, second, left, right)


def pair_sum(value, axis, size, bit=1):
    while bit < size:
        value = value + lax.ppermute(value, axis, [(i, i ^ bit) for i in range(size)])
        bit *= 2
    return value


def all_sketches(inputs, out_grads, first, second, left, right, hops, gathers):
    chips = lax.axis_size("col") // CORES
    me = lax.axis_index("col")
    z, core = me // CORES, me % CORES
    slots = [lax.rem(z - j + chips, chips) * CORES + c for c in (core, 1 - core) for j in range(chips)]
    slots = jnp.stack(slots).astype(jnp.int32)
    starts, rest = [], 0
    for rows in hops + gathers:
        starts.append(rest)
        rest += rows
    sources = [inputs[:, :, s : s + rows] for s, rows in zip(starts, hops + gathers)]
    n = len(hops)

    def hop(value, way, first_chip):
        pairs = []
        for a in range(first_chip, chips - 1):
            a, b = (a, a + 1) if way > 0 else (chips - 1 - a, chips - 2 - a)
            pairs += [(a * CORES + c, b * CORES + c) for c in range(CORES)]
        return lax.ppermute(value, "col", pairs)

    def swap(value):
        return lax.ppermute(value, "col", [(i, i ^ 1) for i in range(chips * CORES)])

    def sketch_of(start, rows, blocks):
        return piece_sketch(
            slots, blocks, out_grads, first, second, left, right, start, rows
        )

    arrived, swapped = [], []
    if n > 0:
        sibling = swap(inputs)
    for k in range(n):
        ups, downs = [sources[k]], [sources[k]]
        for d in range(chips - 1):
            ups.append(hop(ups[-1], 1, d))
            downs.append(hop(downs[-1], -1, d))
        others = jnp.stack(
            [jnp.where(z >= j, ups[j], downs[chips - j]) for j in range(1, chips)]
        )
        if k == 0:
            others, *sources[n:] = lax.optimization_barrier((others, *sources[n:]))
        arrived.append(others)
        swapped.append(swap(others))
    if n > 0:
        *arrived, sources[n] = lax.optimization_barrier((*arrived, sources[n]))
    parts, gathered = [], []
    if n > 0:
        parts.append(sketch_of(0, sum(hops), [inputs, sibling, *arrived, *swapped]))
    if n > 0:
        parts[0], sources[n + 1] = lax.optimization_barrier((parts[0], sources[n + 1]))
    else:
        left, sources[1] = lax.optimization_barrier((left, sources[1]))
    for k in range(n, len(sources)):
        if k >= max(2, n + 2):
            gathered[k - n - 2], sources[k] = lax.optimization_barrier(
                (gathered[k - n - 2], sources[k])
            )
        gathered.append(lax.all_gather(sources[k], "col", axis=1, tiled=True))
    for k, whole in zip(range(n, len(sources)), gathered):
        if parts:
            parts[-1], whole = lax.optimization_barrier((parts[-1], whole))
        parts.append(sketch_of(starts[k], gathers[k - n], [whole]))
    return parts


def body(
    inputs,
    out_grads,
    first_moment,
    second_moment,
    signs_in,
    signs_out,
    rows_in,
    rows_out,
    task_ids,
    weights,
):
    width, local_cols = first_moment.shape
    n_col = lax.axis_size("col")
    n_grp = lax.axis_size("grp")
    me_col = lax.axis_index("col")
    left = signed_hadamard(
        rows_in[:, None], jnp.arange(width, dtype=jnp.int32)[None, :], signs_in[None, :]
    )
    offset = me_col * local_cols
    mine = offset + jnp.arange(local_cols, dtype=jnp.int32)
    signs_mine = lax.dynamic_slice_in_dim(signs_out, offset, local_cols, 0)
    right = signed_hadamard(rows_out[None, :], mine[:, None], signs_mine[:, None])
    sixteenth = width // 16
    hops, gathers = [], [8 * sixteenth, 6 * sixteenth, 2 * sixteenth]
    if n_col == 4 * CORES and inputs.shape[1] % 16 == 0:
        hops, gathers = [2 * sixteenth] * 4, [6 * sixteenth, 2 * sixteenth]
    sketch = sum(
        all_sketches(inputs, out_grads, first_moment, second_moment, left, right, hops, gathers)
    )
    examples, n_left, n_right = sketch.shape
    owned = n_left // n_col
    sketch = sketch + lax.ppermute(sketch, "col", [(i, i ^ 1) for i in range(n_col)])
    sketch = sketch.reshape(examples, n_col // 2, 2, owned, n_right)
    sketch = lax.dynamic_index_in_dim(sketch, me_col % 2, 2, keepdims=False)
    sketch = pair_sum(sketch, "col", n_col, 2)
    squares = jnp.sum(sketch * sketch, axis=(1, 2, 3))
    squares = squares + lax.ppermute(squares, "col", [(i, i ^ 1) for i in range(n_col)])
    unit = lax.dynamic_index_in_dim(sketch, me_col // 2, 1, keepdims=False)
    unit = unit * lax.rsqrt(squares / (n_left * n_right) + 1e-06)[:, None, None]
    protos = jnp.arange(PRO_GRP * n_grp, dtype=jnp.int32)
    coef = jnp.where(
        task_ids[:, None] == protos[None, :], weights[:, None].astype(jnp.float32), 0.0
    )
    term = jnp.sum(coef[:, :, None, None] * unit[:, None], axis=0)
    term = pair_sum(term, "grp", n_grp)
    return lax.dynamic_slice_in_dim(term, lax.axis_index("grp") * PRO_GRP, PRO_GRP, 0)


def solution(mesh):
    placed = (
        P("grp", "col", None),
        P("grp", None, "col"),
        P(None, "col"),
        P(None, "col"),
        P(),
        P(),
        P(),
        P(),
        P("grp"),
        P("grp"),
    )
    return jax.shard_map(
        body, mesh=mesh, in_specs=placed, out_specs=P("grp", "col", None), check_vma=False
    )
```

profile of v0, /device:TPU:0, one launch (start us, length us, event | category | flops | bytes accessed | tf_op | source)
XLA Modules:
  0.0 306.1 jit_solution(17367238300369774132)
XLA Ops:
  6.5 2.6 fusion.1
  10.4 5.6 %collective-permute-start.13 = (bf16[6,32,1024]{2,1,0:T(8,128)(2,1)S(1)}, bf16[6,32,1024]{2,1,0:T(8,128)(2,1)S(1)}, u32[]{:S(2)}, u32[]{:S(2)}) collective-permute-start(bf16[6,32,1024]{2,1,0:T(8,128)(2,1)S(1)} %get-tuple-element.36), channel_id=1, source_target_pairs={{0,2},{1,3},{2,4},{3,5},{4,6},{5,7},{8,10},{9,11},{10,12},{11,13},... | collective-permute-start | bytes 1179656 | tf_op jit(solution)/shard_map/ppermute | solution.py:184
  17.3 4.6 %collective-permute-start.19 = (bf16[6,32,1024]{2,1,0:T(8,128)(2,1)S(1)}, bf16[6,32,1024]{2,1,0:T(8,128)(2,1)S(1)}, u32[]{:S(2)}, u32[]{:S(2)}) collective-permute-start(bf16[6,32,1024]{2,1,0:T(8,128)(2,1)S(1)} %get-tuple-element.35), channel_id=1, source_target_pairs={{0,2},{1,3},{2,4},{3,5},{4,6},{5,7},{8,10},{9,11},{10,12},{11,13},... | collective-permute-start | bytes 1179656 | tf_op jit(solution)/shard_map/ppermute | solution.py:184
  21.9 3.9 %collective-permute-start.7 = (bf16[6,32,1024]{2,1,0:T(8,128)(2,1)}, bf16[6,32,1024]{2,1,0:T(8,128)(2,1)S(1)}, u32[]{:S(2)}, u32[]{:S(2)}) collective-permute-start(bf16[6,32,1024]{2,1,0:T(8,128)(2,1)} %get-tuple-element.37), channel_id=1, source_target_pairs={{0,2},{1,3},{2,4},{3,5},{4,6},{5,7},{8,10},{9,11},{10,12},{11,13},... | collective-permute-start | bytes 1179656 | tf_op jit(solution)/shard_map/ppermute | solution.py:184
  27.1 4.6 %collective-permute-start.1 = (bf16[6,32,1024]{2,1,0:T(8,128)(2,1)S(1)}, bf16[6,32,1024]{2,1,0:T(8,128)(2,1)S(1)}, u32[]{:S(2)}, u32[]{:S(2)}) collective-permute-start(bf16[6,32,1024]{2,1,0:T(8,128)(2,1)S(1)} %get-tuple-element.39), channel_id=1, source_target_pairs={{0,2},{1,3},{2,4},{3,5},{4,6},{5,7},{8,10},{9,11},{10,12},{11,13},... | collective-permute-start | bytes 1179656 | tf_op jit(solution)/shard_map/ppermute | solution.py:184
  35.3 7.1 %collective-permute-done.7 = bf16[6,32,1024]{2,1,0:T(8,128)(2,1)S(1)} collective-permute-done((bf16[6,32,1024]{2,1,0:T(8,128)(2,1)}, bf16[6,32,1024]{2,1,0:T(8,128)(2,1)S(1)}, u32[]{:S(2)}, u32[]{:S(2)}) %collective-permute-start.7) | collective-permute-done | bytes 393248 | tf_op jit(solution)/shard_map/ppermute | solution.py:184
  45.0 4.6 %collective-permute-done.1 = bf16[6,32,1024]{2,1,0:T(8,128)(2,1)S(1)} collective-permute-done((bf16[6,32,1024]{2,1,0:T(8,128)(2,1)S(1)}, bf16[6,32,1024]{2,1,0:T(8,128)(2,1)S(1)}, u32[]{:S(2)}, u32[]{:S(2)}) %collective-permute-start.1) | collective-permute-done | bytes 393248 | tf_op jit(solution)/shard_map/ppermute | solution.py:184
  51.0 2.4 slice.19
  59.1 7.1 %collective-permute-done.3 = bf16[6,32,1024]{2,1,0:T(8,128)(2,1)} collective-permute-done((bf16[6,32,1024]{2,1,0:T(8,128)(2,1)S(1)}, bf16[6,32,1024]{2,1,0:T(8,128)(2,1)}, u32[]{:S(2)}, u32[]{:S(2)}) %collective-permute-start.3) | collective-permute-done | bytes 393248 | tf_op jit(solution)/shard_map/ppermute | solution.py:184
  70.0 4.7 %collective-permute-done.21 = bf16[6,32,1024]{2,1,0:T(8,128)(2,1)} collective-permute-done((bf16[6,32,1024]{2,1,0:T(8,128)(2,1)S(1)}, bf16[6,32,1024]{2,1,0:T(8,128)(2,1)}, u32[]{:S(2)}, u32[]{:S(2)}) %collective-permute-start.21) | collective-permute-done | bytes 393248 | tf_op jit(solution)/shard_map/ppermute | solution.py:184
  79.8 3.2 %collective-permute-done.9 = bf16[6,32,1024]{2,1,0:T(8,128)(2,1)} collective-permute-done((bf16[6,32,1024]{2,1,0:T(8,128)(2,1)S(1)}, bf16[6,32,1024]{2,1,0:T(8,128)(2,1)}, u32[]{:S(2)}, u32[]{:S(2)}) %collective-permute-start.9) | collective-permute-done | bytes 393248 | tf_op jit(solution)/shard_map/ppermute | solution.py:184
  85.5 13.4 %collective-permute-done.4 = bf16[6,32,1024]{2,1,0:T(8,128)(2,1)S(1)} collective-permute-done((bf16[6,32,1024]{2,1,0:T(8,128)(2,1)}, bf16[6,32,1024]{2,1,0:T(8,128)(2,1)S(1)}, u32[]{:S(2)}, u32[]{:S(2)}) %collective-permute-start.4) | collective-permute-done | bytes 393248 | tf_op jit(solution)/shard_map/ppermute | solution.py:184
  106.6 6.6 %collective-permute-done.22 = bf16[6,32,1024]{2,1,0:T(8,128)(2,1)} collective-permute-done((bf16[6,32,1024]{2,1,0:T(8,128)(2,1)}, bf16[6,32,1024]{2,1,0:T(8,128)(2,1)}, u32[]{:S(2)}, u32[]{:S(2)}) %collective-permute-start.22) | collective-permute-done | bytes 393248 | tf_op jit(solution)/shard_map/ppermute | solution.py:184
  115.5 4.3 %collective-permute-done.10 = bf16[6,32,1024]{2,1,0:T(8,128)(2,1)S(1)} collective-permute-done((bf16[6,32,1024]{2,1,0:T(8,128)(2,1)}, bf16[6,32,1024]{2,1,0:T(8,128)(2,1)S(1)}, u32[]{:S(2)}, u32[]{:S(2)}) %collective-permute-start.10) | collective-permute-done | bytes 393248 | tf_op jit(solution)/shard_map/ppermute | solution.py:184
  124.0 5.3 %collective-permute-done.27.refs_8_ = bf16[3,6,32,1024]{3,2,1,0:T(8,128)(2,1)S(1)} collective-permute-done((bf16[3,6,32,1024]{3,2,1,0:T(8,128)(2,1)S(1)}, bf16[3,6,32,1024]{3,2,1,0:T(8,128)(2,1)S(1)}, u32[]{:S(2)}, u32[]{:S(2)}) %collective-permute-start.27) | collective-permute-done | bytes 1179680 | tf_op jit(solution)/shard_map/ppermute | solution.py:187
  137.7 52.2 %piece_sketch.3 = f32[6,64,128]{2,1,0:T(8,128)S(1)} custom-call(s32[8]{0:T(128)S(1)} %stack.83.slots_ref, bf16[6,32,8192]{2,1,0:T(8,128)(2,1)} %refs_0_.1, bf16[6,32,8192]{2,1,0:T(8,128)(2,1)} %collective-permute-done.refs_1_, bf16[3,6,32,1024]{3,2,1,0:T(8,128)(2,1)S(1)} %copy-done.5, bf16[3,6,32,1024]{3,2,1,0:T(8,128)(2,1)S(1)} %copy-done.9, ...), custom_call_target="tpu_custom_call" | custom-call | flops 1 | bytes 1 | tf_op jit(solution)/shard_map/piece_sketch/pallas_call | solution.py:131
  191.5 23.4 %all-gather.3.cloned.1.call-done.refs_0_ = bf16[6,256,3072]{2,1,0:T(8,128)(2,1)} async-done(((bf16[6,32,3072]{2,1,0:T(8,128)(2,1)}), bf16[6,256,3072]{2,1,0:T(8,128)(2,1)}) %all-gather.3.cloned.1.call-update) | async-done | bytes 9437200 | tf_op jit(solution)/shard_map/all_gather | solution.py:223
  217.2 39.0 %piece_sketch.4 = f32[6,64,128]{2,1,0:T(8,128)S(1)} custom-call(s32[8]{0:T(128)S(1)} %stack.83.slots_ref, bf16[6,256,3072]{2,1,0:T(8,128)(2,1)} %all-gather.3.cloned.1.call-done.refs_0_, bf16[6,256,1024]{2,1,0:T(8,128)(2,1)S(1)} %copy-done, f32[8192,1024]{1,0:T(8,128)} %refs_2_.3, f32[8192,1024]{1,0:T(8,128)} %refs_3_.3, bf16[64,8192]{1,0:T(8,128)(2,1)S(1)} %copy-done.2, ...), custom_call_target="tpu_custom_call" | custom-call | flops 1 | bytes 1 | tf_op jit(solution)/shard_map/piece_sketch/pallas_call | solution.py:131
  258.1 1.9 copy-done.13
  260.0 15.4 %piece_sketch.5 = f32[6,64,128]{2,1,0:T(8,128)S(1)} custom-call(s32[8]{0:T(128)S(1)} %stack.83.slots_ref, bf16[6,256,1024]{2,1,0:T(8,128)(2,1)S(1)} %copy-done.13, bf16[6,256,1024]{2,1,0:T(8,128)(2,1)} %refs_1_.3, f32[8192,1024]{1,0:T(8,128)} %refs_2_.3, f32[8192,1024]{1,0:T(8,128)} %refs_3_.3, bf16[64,8192]{1,0:T(8,128)(2,1)S(1)} %copy-done.3, ...), custom_call_target="tpu_custom_call" | custom-call | flops 1 | bytes 1 | tf_op jit(solution)/shard_map/piece_sketch/pallas_call | solution.py:131
  277.1 4.9 %collective-permute-done.30 = f32[6,4,8,128]{3,2,1,0:T(8,128)S(1)} collective-permute-done((f32[6,4,8,128]{3,2,1,0:T(8,128)S(1)}, f32[6,4,8,128]{3,2,1,0:T(8,128)S(1)}, u32[]{:S(2)}, u32[]{:S(2)}) %collective-permute-start.30) | collective-permute-done | bytes 98336 | tf_op jit(solution)/shard_map/ppermute | solution.py:161
  283.1 6.2 %collective-permute-done.31 = f32[6,4,8,128]{3,2,1,0:T(8,128)S(1)} collective-permute-done((f32[6,4,8,128]{3,2,1,0:T(8,128)S(1)}, f32[6,4,8,128]{3,2,1,0:T(8,128)S(1)}, u32[]{:S(2)}, u32[]{:S(2)}) %collective-permute-start.31) | collective-permute-done | bytes 98336 | tf_op jit(solution)/shard_map/ppermute | solution.py:161
  292.3 2.4 collective-permute-done.33
  296.3 2.4 collective-permute-done.34
  (170 shorter events, 64.1 us)
Async XLA Ops:
  6.5 208.4 %all-gather.3.cloned.1.call-start = ((), (), s32[]{:S(2)}) async-start(), calls=%async_computation | async-start | bytes 10616832 | tf_op jit(solution)/shard_map/all_gather | solution.py:223
  9.1 16.7 %collective-permute-start.14 = (bf16[6,32,1024]{2,1,0:T(8,128)(2,1)S(1)}, bf16[6,32,1024]{2,1,0:T(8,128)(2,1)S(1)}, u32[]{:S(2)}, u32[]{:S(2)}) collective-permute-start(bf16[6,32,1024]{2,1,0:T(8,128)(2,1)S(1)} %get-tuple-element.36), channel_id=1, source_target_pairs={{6,4},{7,5},{4,2},{5,3},{2,0},{3,1},{14,12},{15,13},{12,10},{13,11... | collective-permute-start | bytes 1179656 | tf_op jit(solution)/shard_map/ppermute | solution.py:184
  10.4 16.7 %collective-permute-start.13 = (bf16[6,32,1024]{2,1,0:T(8,128)(2,1)S(1)}, bf16[6,32,1024]{2,1,0:T(8,128)(2,1)S(1)}, u32[]{:S(2)}, u32[]{:S(2)}) collective-permute-start(bf16[6,32,1024]{2,1,0:T(8,128)(2,1)S(1)} %get-tuple-element.36), channel_id=1, source_target_pairs={{0,2},{1,3},{2,4},{3,5},{4,6},{5,7},{8,10},{9,11},{10,12},{11,13},... | collective-permute-start | bytes 1179656 | tf_op jit(solution)/shard_map/ppermute | solution.py:184
  16.0 16.4 %collective-permute-start.20 = (bf16[6,32,1024]{2,1,0:T(8,128)(2,1)S(1)}, bf16[6,32,1024]{2,1,0:T(8,128)(2,1)S(1)}, u32[]{:S(2)}, u32[]{:S(2)}) collective-permute-start(bf16[6,32,1024]{2,1,0:T(8,128)(2,1)S(1)} %get-tuple-element.35), channel_id=1, source_target_pairs={{6,4},{7,5},{4,2},{5,3},{2,0},{3,1},{14,12},{15,13},{12,10},{13,11... | collective-permute-start | bytes 1179656 | tf_op jit(solution)/shard_map/ppermute | solution.py:184
  17.3 16.6 %collective-permute-start.19 = (bf16[6,32,1024]{2,1,0:T(8,128)(2,1)S(1)}, bf16[6,32,1024]{2,1,0:T(8,128)(2,1)S(1)}, u32[]{:S(2)}, u32[]{:S(2)}) collective-permute-start(bf16[6,32,1024]{2,1,0:T(8,128)(2,1)S(1)} %get-tuple-element.35), channel_id=1, source_target_pairs={{0,2},{1,3},{2,4},{3,5},{4,6},{5,7},{8,10},{9,11},{10,12},{11,13},... | collective-permute-start | bytes 1179656 | tf_op jit(solution)/shard_map/ppermute | solution.py:184
  21.9 20.6 %collective-permute-start.7 = (bf16[6,32,1024]{2,1,0:T(8,128)(2,1)}, bf16[6,32,1024]{2,1,0:T(8,128)(2,1)S(1)}, u32[]{:S(2)}, u32[]{:S(2)}) collective-permute-start(bf16[6,32,1024]{2,1,0:T(8,128)(2,1)} %get-tuple-element.37), channel_id=1, source_target_pairs={{0,2},{1,3},{2,4},{3,5},{4,6},{5,7},{8,10},{9,11},{10,12},{11,13},... | collective-permute-start | bytes 1179656 | tf_op jit(solution)/shard_map/ppermute | solution.py:184
  25.8 17.9 %collective-permute-start.2 = (bf16[6,32,1024]{2,1,0:T(8,128)(2,1)S(1)}, bf16[6,32,1024]{2,1,0:T(8,128)(2,1)S(1)}, u32[]{:S(2)}, u32[]{:S(2)}) collective-permute-start(bf16[6,32,1024]{2,1,0:T(8,128)(2,1)S(1)} %get-tuple-element.39), channel_id=1, source_target_pairs={{6,4},{7,5},{4,2},{5,3},{2,0},{3,1},{14,12},{15,13},{12,10},{13,11... | collective-permute-start | bytes 1179656 | tf_op jit(solution)/shard_map/ppermute | solution.py:184
  27.1 22.5 %collective-permute-start.1 = (bf16[6,32,1024]{2,1,0:T(8,128)(2,1)S(1)}, bf16[6,32,1024]{2,1,0:T(8,128)(2,1)S(1)}, u32[]{:S(2)}, u32[]{:S(2)}) collective-permute-start(bf16[6,32,1024]{2,1,0:T(8,128)(2,1)S(1)} %get-tuple-element.39), channel_id=1, source_target_pairs={{0,2},{1,3},{2,4},{3,5},{4,6},{5,7},{8,10},{9,11},{10,12},{11,13},... | collective-permute-start | bytes 1179656 | tf_op jit(solution)/shard_map/ppermute | solution.py:184
  32.4 21.0 %collective-permute-start.15 = (bf16[6,32,1024]{2,1,0:T(8,128)(2,1)S(1)}, bf16[6,32,1024]{2,1,0:T(8,128)(2,1)}, u32[]{:S(2)}, u32[]{:S(2)}) collective-permute-start(bf16[6,32,1024]{2,1,0:T(8,128)(2,1)S(1)} %collective-permute-done.14), channel_id=1, source_target_pairs={{4,2},{5,3},{2,0},{3,1},{12,10},{13,11},{10,8},{11,9},{20,18},{21,... | collective-permute-start | bytes 1179656 | tf_op jit(solution)/shard_map/ppermute | solution.py:184
  33.9 20.9 %collective-permute-start.17 = (bf16[6,32,1024]{2,1,0:T(8,128)(2,1)S(1)}, bf16[6,32,1024]{2,1,0:T(8,128)(2,1)}, u32[]{:S(2)}, u32[]{:S(2)}) collective-permute-start(bf16[6,32,1024]{2,1,0:T(8,128)(2,1)S(1)} %collective-permute-done.13), channel_id=1, source_target_pairs={{2,4},{3,5},{4,6},{5,7},{10,12},{11,13},{12,14},{13,15},{18,20},{1... | collective-permute-start | bytes 1179656 | tf_op jit(solution)/shard_map/ppermute | solution.py:184
  42.4 15.2 %collective-permute-start.8 = (bf16[6,32,1024]{2,1,0:T(8,128)(2,1)}, bf16[6,32,1024]{2,1,0:T(8,128)(2,1)S(1)}, u32[]{:S(2)}, u32[]{:S(2)}) collective-permute-start(bf16[6,32,1024]{2,1,0:T(8,128)(2,1)} %get-tuple-element.37), channel_id=1, source_target_pairs={{6,4},{7,5},{4,2},{5,3},{2,0},{3,1},{14,12},{15,13},{12,10},{13,11... | collective-permute-start | bytes 1179656 | tf_op jit(solution)/shard_map/ppermute | solution.py:184
  43.7 22.5 %collective-permute-start.3 = (bf16[6,32,1024]{2,1,0:T(8,128)(2,1)S(1)}, bf16[6,32,1024]{2,1,0:T(8,128)(2,1)}, u32[]{:S(2)}, u32[]{:S(2)}) collective-permute-start(bf16[6,32,1024]{2,1,0:T(8,128)(2,1)S(1)} %collective-permute-done.2), channel_id=1, source_target_pairs={{4,2},{5,3},{2,0},{3,1},{12,10},{13,11},{10,8},{11,9},{20,18},{21,... | collective-permute-start | bytes 1179656 | tf_op jit(solution)/shard_map/ppermute | solution.py:184
  49.6 17.9 %collective-permute-start.5 = (bf16[6,32,1024]{2,1,0:T(8,128)(2,1)S(1)}, bf16[6,32,1024]{2,1,0:T(8,128)(2,1)}, u32[]{:S(2)}, u32[]{:S(2)}) collective-permute-start(bf16[6,32,1024]{2,1,0:T(8,128)(2,1)S(1)} %collective-permute-done.1), channel_id=1, source_target_pairs={{2,4},{3,5},{4,6},{5,7},{10,12},{11,13},{12,14},{13,15},{18,20},{1... | collective-permute-start | bytes 1179656 | tf_op jit(solution)/shard_map/ppermute | solution.py:184
  53.4 21.2 %collective-permute-start.21 = (bf16[6,32,1024]{2,1,0:T(8,128)(2,1)S(1)}, bf16[6,32,1024]{2,1,0:T(8,128)(2,1)}, u32[]{:S(2)}, u32[]{:S(2)}) collective-permute-start(bf16[6,32,1024]{2,1,0:T(8,128)(2,1)S(1)} %collective-permute-done.20), channel_id=1, source_target_pairs={{4,2},{5,3},{2,0},{3,1},{12,10},{13,11},{10,8},{11,9},{20,18},{21,... | collective-permute-start | bytes 1179656 | tf_op jit(solution)/shard_map/ppermute | solution.py:184
  54.8 21.1 %collective-permute-start.23 = (bf16[6,32,1024]{2,1,0:T(8,128)(2,1)S(1)}, bf16[6,32,1024]{2,1,0:T(8,128)(2,1)}, u32[]{:S(2)}, u32[]{:S(2)}) collective-permute-start(bf16[6,32,1024]{2,1,0:T(8,128)(2,1)S(1)} %collective-permute-done.19), channel_id=1, source_target_pairs={{2,4},{3,5},{4,6},{5,7},{10,12},{11,13},{12,14},{13,15},{18,20},{1... | collective-permute-start | bytes 1179656 | tf_op jit(solution)/shard_map/ppermute | solution.py:184
  57.7 20.6 %collective-permute-start.11 = (bf16[6,32,1024]{2,1,0:T(8,128)(2,1)S(1)}, bf16[6,32,1024]{2,1,0:T(8,128)(2,1)}, u32[]{:S(2)}, u32[]{:S(2)}) collective-permute-start(bf16[6,32,1024]{2,1,0:T(8,128)(2,1)S(1)} %collective-permute-done.7), channel_id=1, source_target_pairs={{2,4},{3,5},{4,6},{5,7},{10,12},{11,13},{12,14},{13,15},{18,20},{1... | collective-permute-start | bytes 1179656 | tf_op jit(solution)/shard_map/ppermute | solution.py:184
  66.2 16.9 %collective-permute-start.9 = (bf16[6,32,1024]{2,1,0:T(8,128)(2,1)S(1)}, bf16[6,32,1024]{2,1,0:T(8,128)(2,1)}, u32[]{:S(2)}, u32[]{:S(2)}) collective-permute-start(bf16[6,32,1024]{2,1,0:T(8,128)(2,1)S(1)} %collective-permute-done.8), channel_id=1, source_target_pairs={{4,2},{5,3},{2,0},{3,1},{12,10},{13,11},{10,8},{11,9},{20,18},{21,... | collective-permute-start | bytes 1179656 | tf_op jit(solution)/shard_map/ppermute | solution.py:184
  67.5 34.5 %collective-permute-start.18 = (bf16[6,32,1024]{2,1,0:T(8,128)(2,1)}, bf16[6,32,1024]{2,1,0:T(8,128)(2,1)}, u32[]{:S(2)}, u32[]{:S(2)}) collective-permute-start(bf16[6,32,1024]{2,1,0:T(8,128)(2,1)} %collective-permute-done.17), channel_id=1, source_target_pairs={{4,6},{5,7},{12,14},{13,15},{20,22},{21,23},{28,30},{29,31}} | collective-permute-start | bytes 1179656 | tf_op jit(solution)/shard_map/ppermute | solution.py:184
  74.6 29.8 %collective-permute-start.16 = (bf16[6,32,1024]{2,1,0:T(8,128)(2,1)}, bf16[6,32,1024]{2,1,0:T(8,128)(2,1)}, u32[]{:S(2)}, u32[]{:S(2)}) collective-permute-start(bf16[6,32,1024]{2,1,0:T(8,128)(2,1)} %collective-permute-done.15), channel_id=1, source_target_pairs={{2,0},{3,1},{10,8},{11,9},{18,16},{19,17},{26,24},{27,25}} | collective-permute-start | bytes 1179656 | tf_op jit(solution)/shard_map/ppermute | solution.py:184
  75.9 23.0 %collective-permute-start.4 = (bf16[6,32,1024]{2,1,0:T(8,128)(2,1)}, bf16[6,32,1024]{2,1,0:T(8,128)(2,1)S(1)}, u32[]{:S(2)}, u32[]{:S(2)}) collective-permute-start(bf16[6,32,1024]{2,1,0:T(8,128)(2,1)} %collective-permute-done.3), channel_id=1, source_target_pairs={{2,0},{3,1},{10,8},{11,9},{18,16},{19,17},{26,24},{27,25}} | collective-permute-start | bytes 1179656 | tf_op jit(solution)/shard_map/ppermute | solution.py:184
  78.3 27.4 %collective-permute-start.24 = (bf16[6,32,1024]{2,1,0:T(8,128)(2,1)}, bf16[6,32,1024]{2,1,0:T(8,128)(2,1)}, u32[]{:S(2)}, u32[]{:S(2)}) collective-permute-start(bf16[6,32,1024]{2,1,0:T(8,128)(2,1)} %collective-permute-done.23), channel_id=1, source_target_pairs={{4,6},{5,7},{12,14},{13,15},{20,22},{21,23},{28,30},{29,31}} | collective-permute-start | bytes 1179656 | tf_op jit(solution)/shard_map/ppermute | solution.py:184
  83.0 17.3 %collective-permute-start.6 = (bf16[6,32,1024]{2,1,0:T(8,128)(2,1)}, bf16[6,32,1024]{2,1,0:T(8,128)(2,1)S(1)}, u32[]{:S(2)}, u32[]{:S(2)}) collective-permute-start(bf16[6,32,1024]{2,1,0:T(8,128)(2,1)} %collective-permute-done.5), channel_id=1, source_target_pairs={{4,6},{5,7},{12,14},{13,15},{20,22},{21,23},{28,30},{29,31}} | collective-permute-start | bytes 1179656 | tf_op jit(solution)/shard_map/ppermute | solution.py:184
  102.0 17.8 %collective-permute-start.10 = (bf16[6,32,1024]{2,1,0:T(8,128)(2,1)}, bf16[6,32,1024]{2,1,0:T(8,128)(2,1)S(1)}, u32[]{:S(2)}, u32[]{:S(2)}) collective-permute-start(bf16[6,32,1024]{2,1,0:T(8,128)(2,1)} %collective-permute-done.9), channel_id=1, source_target_pairs={{2,0},{3,1},{10,8},{11,9},{18,16},{19,17},{26,24},{27,25}} | collective-permute-start | bytes 1179656 | tf_op jit(solution)/shard_map/ppermute | solution.py:184
  120.0 136.8 %all-gather.5.cloned.1.call-start = ((), (), s32[]{:S(2)}) async-start(), calls=%async_computation.1 | async-start | bytes 3538944 | tf_op jit(solution)/shard_map/all_gather | solution.py:223
  (53 other events, 533.0 us)
Sparse Core Ops, SparseCore 0:
  120.2 94.7 all-gather.2
  216.6 36.7 all-gather.4
where the time goes:
time: 307 us; the launch traced here: 306 us
  Pallas kernels  107 us (35%)
  waiting for transfers between devices  103 us (34%)
  starting transfers between devices  50.7 us (17%)
  local copies, waits for them, and re-layouts  19.2 us (6%)
  between operations  14.2 us (5%)
  other arithmetic  12.6 us (4%)
    pallas_call x3, Pallas kernels, piece_sketch(): pl.pallas_call(functools.partial(sketch_kernel, len(parts), per), grid=(r...  107 us
    ppermute x24, waiting for transfers between devices, hop(): return lax.ppermute(value, 'col', pairs)  52.4 us
    ppermute x24, starting transfers between devices, hop(): return lax.ppermute(value, 'col', pairs)  44.9 us
    all_gather x2, waiting for transfers between devices, all_sketches(): gathered.append(lax.all_gather(sources[k], 'col', axis=1, tiled=True))  23.4 us
    ppermute x4, waiting for transfers between devices, pair_sum(): lax.ppermute(value, axis, [(i, i ^ bit) for i in range(size)])  16 us
    unnamed x80, local copies, waits for them, and re-layouts  13.4 us
    another operation x16, other arithmetic, all_sketches(): jnp.stack([jnp.where(z >= j, ups[j], downs[chips - j]) for j in range(1,...  9.87 us
    ppermute x5, waiting for transfers between devices, swap(): lax.ppermute(value, 'col', [(i, i ^ 1) for i in range(chips * CORES)])  8.71 us
  transfers between devices with their start and end apart: 37, of which 22 were waited for; matrix products, arithmetic and copies ran while one was open for 5% of the time, Pallas kernels for 30%

commit v1 on v0

--- a/solution.py
+++ b/solution.py
@@ -149,7 +149,7 @@
         + [pltpu.VMEM((block, cols), jnp.bfloat16)] * 2
         + [pltpu.VMEM((block, n_right), jnp.float32)] * 2,
         compiler_params=pltpu.CompilerParams(
-            vmem_limit_bytes=48 * 1024 * 1024, dimension_semantics=("arbitrary",)
+            vmem_limit_bytes=(60 if rows <= 2 * block else 48) * 1024 * 1024, dimension_semantics=("arbitrary",)
         ),
         cost_estimate=pl.CostEstimate(flops=1, bytes_accessed=1, transcendentals=0),
         name="piece_sketch",
@@ -254,7 +254,7 @@
     sixteenth = width // 16
     hops, gathers = [], [8 * sixteenth, 6 * sixteenth, 2 * sixteenth]
     if n_col == 4 * CORES and inputs.shape[1] % 16 == 0:
-        hops, gathers = [2 * sixteenth] * 4, [6 * sixteenth, 2 * sixteenth]
+        hops, gathers = [3 * sixteenth] * 3, [5 * sixteenth, 2 * sixteenth]
     sketch = sum(
         all_sketches(inputs, out_grads, first_moment, second_moment, left, right, hops, gathers)
     )
@@ -273,8 +273,12 @@
         task_ids[:, None] == protos[None, :], weights[:, None].astype(jnp.float32), 0.0
     )
     term = jnp.sum(coef[:, :, None, None] * unit[:, None], axis=0)
-    term = pair_sum(term, "grp", n_grp)
-    return lax.dynamic_slice_in_dim(term, lax.axis_index("grp") * PRO_GRP, PRO_GRP, 0)
+    me_grp = lax.axis_index("grp")
+    total = lax.dynamic_slice_in_dim(term, me_grp * PRO_GRP, PRO_GRP, 0)
+    for d in range(1, n_grp):
+        theirs = lax.dynamic_slice_in_dim(term, jnp.bitwise_xor(me_grp, d) * PRO_GRP, PRO_GRP, 0)
+        total = total + lax.ppermute(theirs, "grp", [(i, i ^ d) for i in range(n_grp)])
+    return total
 
 
 def solution(mesh):

time: 307 us -> 299 us (0.974)
  waiting for transfers between devices: 103 us -> 116 us
  starting transfers between devices: 50.7 us -> 37.8 us
  local copies, waits for them, and re-layouts: 19.2 us -> 14.6 us
  other arithmetic: 12.6 us -> 8.4 us
    ppermute x24 -> x18, waiting for transfers between devices: 52.4 us -> 80.9 us  [hop(): return lax.ppermute(value, 'col', pairs)]
    all_gather x2, waiting for transfers between devices: 23.4 us -> 8.51 us  [all_sketches(): gathered.append(lax.all_gather(sources[k], 'col', axis=1, tiled=True))]
    ppermute x24 -> x18, starting transfers between devices: 44.9 us -> 30.8 us  [hop(): return lax.ppermute(value, 'col', pairs)]
    ppermute x4 -> x2, waiting for transfers between devices: 16 us -> 10.2 us  [pair_sum(): lax.ppermute(value, axis, [(i, i ^ bit) for i in range(size)])]
    another operation x16 -> x12, other arithmetic: 9.87 us -> 4.69 us  [all_sketches(): jnp.stack([jnp.where(z >= j, ups[j], downs[chips - j]) for j in range(1,...]
    unnamed x80 -> x38, local copies, waits for them, and re-layouts: 13.4 us -> 8.25 us
    ppermute x0 -> x3, waiting for transfers between devices: none -> 4.01 us  [body(): lax.ppermute(theirs, 'grp', [(i, i ^ d) for i in range(n_grp)])]
    ppermute x0 -> x3, starting transfers between devices: none -> 3.55 us  [body(): lax.ppermute(theirs, 'grp', [(i, i ^ d) for i in range(n_grp)])]
  transfers between devices with their start and end apart: 37 -> 31, of which waited for: 22 -> 20; matrix products, arithmetic and copies ran while one was open for 5% -> 4% of each run, Pallas kernels for 30% -> 30%
where the time goes in v1:
time: 299 us; the launch traced here: 298 us
  waiting for transfers between devices  116 us (39%)
  Pallas kernels  108 us (36%)
  starting transfers between devices  37.8 us (13%)
  local copies, waits for them, and re-layouts  14.6 us (5%)
  between operations  13.9 us (5%)
  other arithmetic  8.4 us (3%)
    pallas_call x3, Pallas kernels, piece_sketch(): pl.pallas_call(functools.partial(sketch_kernel, len(parts), per), grid=(r...  108 us
    ppermute x18, waiting for transfers between devices, hop(): return lax.ppermute(value, 'col', pairs)  80.9 us
    ppermute x18, starting transfers between devices, hop(): return lax.ppermute(value, 'col', pairs)  30.8 us
    ppermute x2, waiting for transfers between devices, pair_sum(): lax.ppermute(value, axis, [(i, i ^ bit) for i in range(size)])  10.2 us
    ppermute x4, waiting for transfers between devices, swap(): lax.ppermute(value, 'col', [(i, i ^ 1) for i in range(chips * CORES)])  9.65 us
    all_gather x2, waiting for transfers between devices, all_sketches(): gathered.append(lax.all_gather(sources[k], 'col', axis=1, tiled=True))  8.51 us
    unnamed x38, local copies, waits for them, and re-layouts  8.25 us
  transfers between devices with their start and end apart: 31, of which 20 were waited for; matrix products, arithmetic and copies ran while one was open for 4% of the time, Pallas kernels for 30%

profile of v1, /device:TPU:0, one launch (start us, length us, event | category | flops | bytes accessed | tf_op | source)
XLA Modules:
  0.0 298.0 jit_solution(14893634320254546362)
XLA Ops:
  9.4 5.6 %collective-permute-start.13 = (bf16[6,32,1536]{2,1,0:T(8,128)(2,1)S(1)}, bf16[6,32,1536]{2,1,0:T(8,128)(2,1)S(1)}, u32[]{:S(2)}, u32[]{:S(2)}) collective-permute-start(bf16[6,32,1536]{2,1,0:T(8,128)(2,1)S(1)} %get-tuple-element.33), channel_id=1, source_target_pairs={{0,2},{1,3},{2,4},{3,5},{4,6},{5,7},{8,10},{9,11},{10,12},{11,13},... | collective-permute-start | bytes 1769480 | tf_op jit(solution)/shard_map/ppermute | solution.py:184
  15.0 3.9 %collective-permute-start.7 = (bf16[6,32,1536]{2,1,0:T(8,128)(2,1)S(1)}, bf16[6,32,1536]{2,1,0:T(8,128)(2,1)S(1)}, u32[]{:S(2)}, u32[]{:S(2)}) collective-permute-start(bf16[6,32,1536]{2,1,0:T(8,128)(2,1)S(1)} %get-tuple-element.34), channel_id=1, source_target_pairs={{0,2},{1,3},{2,4},{3,5},{4,6},{5,7},{8,10},{9,11},{10,12},{11,13},... | collective-permute-start | bytes 1769480 | tf_op jit(solution)/shard_map/ppermute | solution.py:184
  21.5 5.6 %collective-permute-done.14 = bf16[6,32,1536]{2,1,0:T(8,128)(2,1)S(1)} collective-permute-done((bf16[6,32,1536]{2,1,0:T(8,128)(2,1)S(1)}, bf16[6,32,1536]{2,1,0:T(8,128)(2,1)S(1)}, u32[]{:S(2)}, u32[]{:S(2)}) %collective-permute-start.14) | collective-permute-done | bytes 589856 | tf_op jit(solution)/shard_map/ppermute | solution.py:184
  27.2 4.0 %collective-permute-start.1 = (bf16[6,32,1536]{2,1,0:T(8,128)(2,1)S(1)}, bf16[6,32,1536]{2,1,0:T(8,128)(2,1)S(1)}, u32[]{:S(2)}, u32[]{:S(2)}) collective-permute-start(bf16[6,32,1536]{2,1,0:T(8,128)(2,1)S(1)} %get-tuple-element.35), channel_id=1, source_target_pairs={{0,2},{1,3},{2,4},{3,5},{4,6},{5,7},{8,10},{9,11},{10,12},{11,13},... | collective-permute-start | bytes 1769480 | tf_op jit(solution)/shard_map/ppermute | solution.py:184
  32.5 8.8 %collective-permute-done.7 = bf16[6,32,1536]{2,1,0:T(8,128)(2,1)S(1)} collective-permute-done((bf16[6,32,1536]{2,1,0:T(8,128)(2,1)S(1)}, bf16[6,32,1536]{2,1,0:T(8,128)(2,1)S(1)}, u32[]{:S(2)}, u32[]{:S(2)}) %collective-permute-start.7) | collective-permute-done | bytes 589856 | tf_op jit(solution)/shard_map/ppermute | solution.py:184
  44.3 8.1 %collective-permute-done.2 = bf16[6,32,1536]{2,1,0:T(8,128)(2,1)S(1)} collective-permute-done((bf16[6,32,1536]{2,1,0:T(8,128)(2,1)S(1)}, bf16[6,32,1536]{2,1,0:T(8,128)(2,1)S(1)}, u32[]{:S(2)}, u32[]{:S(2)}) %collective-permute-start.2) | collective-permute-done | bytes 589856 | tf_op jit(solution)/shard_map/ppermute | solution.py:184
  54.6 2.2 slice.16
  56.8 1.8 slice.17
  59.9 5.3 %collective-permute-done.15 = bf16[6,32,1536]{2,1,0:T(8,128)(2,1)} collective-permute-done((bf16[6,32,1536]{2,1,0:T(8,128)(2,1)S(1)}, bf16[6,32,1536]{2,1,0:T(8,128)(2,1)}, u32[]{:S(2)}, u32[]{:S(2)}) %collective-permute-start.15) | collective-permute-done | bytes 589856 | tf_op jit(solution)/shard_map/ppermute | solution.py:184
  69.1 8.8 %collective-permute-done.9 = bf16[6,32,1536]{2,1,0:T(8,128)(2,1)} collective-permute-done((bf16[6,32,1536]{2,1,0:T(8,128)(2,1)S(1)}, bf16[6,32,1536]{2,1,0:T(8,128)(2,1)}, u32[]{:S(2)}, u32[]{:S(2)}) %collective-permute-start.9) | collective-permute-done | bytes 589856 | tf_op jit(solution)/shard_map/ppermute | solution.py:184
  79.7 10.7 %collective-permute-done.3 = bf16[6,32,1536]{2,1,0:T(8,128)(2,1)S(1)} collective-permute-done((bf16[6,32,1536]{2,1,0:T(8,128)(2,1)}, bf16[6,32,1536]{2,1,0:T(8,128)(2,1)S(1)}, u32[]{:S(2)}, u32[]{:S(2)}) %collective-permute-start.3) | collective-permute-done | bytes 589856 | tf_op jit(solution)/shard_map/ppermute | solution.py:184
  93.9 9.1 %collective-permute-done.16 = bf16[6,32,1536]{2,1,0:T(8,128)(2,1)S(1)} collective-permute-done((bf16[6,32,1536]{2,1,0:T(8,128)(2,1)}, bf16[6,32,1536]{2,1,0:T(8,128)(2,1)S(1)}, u32[]{:S(2)}, u32[]{:S(2)}) %collective-permute-start.16) | collective-permute-done | bytes 589856 | tf_op jit(solution)/shard_map/ppermute | solution.py:184
  103.1 24.4 %collective-permute-done.4 = bf16[6,32,1536]{2,1,0:T(8,128)(2,1)S(1)} collective-permute-done((bf16[6,32,1536]{2,1,0:T(8,128)(2,1)S(1)}, bf16[6,32,1536]{2,1,0:T(8,128)(2,1)S(1)}, u32[]{:S(2)}, u32[]{:S(2)}) %collective-permute-start.4) | collective-permute-done | bytes 589856 | tf_op jit(solution)/shard_map/ppermute | solution.py:184
  133.4 2.4 collective-permute-done.refs_1_
  135.8 4.9 %collective-permute-done.21.refs_7_ = bf16[3,6,32,1536]{3,2,1,0:T(8,128)(2,1)S(1)} collective-permute-done((bf16[3,6,32,1536]{3,2,1,0:T(8,128)(2,1)}, bf16[3,6,32,1536]{3,2,1,0:T(8,128)(2,1)S(1)}, u32[]{:S(2)}, u32[]{:S(2)}) %collective-permute-start.21) | collective-permute-done | bytes 1769504 | tf_op jit(solution)/shard_map/ppermute | solution.py:187
  140.8 2.3 collective-permute-done.19.refs_5_
  147.3 57.8 %piece_sketch.3 = f32[6,64,128]{2,1,0:T(8,128)S(1)} custom-call(s32[8]{0:T(128)S(1)} %stack.71.slots_ref, bf16[6,32,8192]{2,1,0:T(8,128)(2,1)} %refs_0_.1, bf16[6,32,8192]{2,1,0:T(8,128)(2,1)} %collective-permute-done.refs_1_, bf16[3,6,32,1536]{3,2,1,0:T(8,128)(2,1)S(1)} %copy-done.4, bf16[3,6,32,1536]{3,2,1,0:T(8,128)(2,1)S(1)} %copy-done.6, ...), custom_call_target="tpu_custom_call" | custom-call | flops 1 | bytes 1 | tf_op jit(solution)/shard_map/piece_sketch/pallas_call | solution.py:131
  206.1 5.2 %all-gather.3.cloned.1.call-done.refs_0_ = bf16[6,256,2560]{2,1,0:T(8,128)(2,1)} async-done(((bf16[6,32,2560]{2,1,0:T(8,128)(2,1)}), bf16[6,256,2560]{2,1,0:T(8,128)(2,1)}) %all-gather.3.cloned.1.call-update) | async-done | bytes 7864336 | tf_op jit(solution)/shard_map/all_gather | solution.py:223
  213.4 32.9 %piece_sketch.4 = f32[6,64,128]{2,1,0:T(8,128)S(1)} custom-call(s32[8]{0:T(128)S(1)} %stack.71.slots_ref, bf16[6,256,2560]{2,1,0:T(8,128)(2,1)} %all-gather.3.cloned.1.call-done.refs_0_, bf16[6,256,1024]{2,1,0:T(8,128)(2,1)S(1)} %copy-done, f32[8192,1024]{1,0:T(8,128)} %refs_2_.3, f32[8192,1024]{1,0:T(8,128)} %refs_3_.3, bf16[64,8192]{1,0:T(8,128)(2,1)S(1)} %copy-done.2, ...), custom_call_target="tpu_custom_call" | custom-call | flops 1 | bytes 1 | tf_op jit(solution)/shard_map/piece_sketch/pallas_call | solution.py:131
  246.4 3.3 %all-gather.5.cloned.1.call-done.refs_0_ = bf16[6,256,1024]{2,1,0:T(8,128)(2,1)} async-done(((bf16[6,32,1024]{2,1,0:T(8,128)(2,1)}), bf16[6,256,1024]{2,1,0:T(8,128)(2,1)}) %all-gather.5.cloned.1.call-update) | async-done | bytes 3145744 | tf_op jit(solution)/shard_map/all_gather | solution.py:223
  249.8 17.0 %piece_sketch.5 = f32[6,64,128]{2,1,0:T(8,128)} custom-call(s32[8]{0:T(128)} %copy-done.9, bf16[6,256,1024]{2,1,0:T(8,128)(2,1)} %all-gather.5.cloned.1.call-done.refs_0_, bf16[6,256,1024]{2,1,0:T(8,128)(2,1)} %refs_1_.3, f32[8192,1024]{1,0:T(8,128)} %refs_2_.3, f32[8192,1024]{1,0:T(8,128)} %refs_3_.3, bf16[64,8192]{1,0:T(8,128)(2,1)} %copy-done.1, ...), custom_call_target="tpu_custom_call" | custom-call | flops 1 | bytes 1 | tf_op jit(solution)/shard_map/piece_sketch/pallas_call | solution.py:131
  269.8 4.4 %collective-permute-done.23 = f32[6,4,8,128]{3,2,1,0:T(8,128)S(1)} collective-permute-done((f32[6,4,8,128]{3,2,1,0:T(8,128)S(1)}, f32[6,4,8,128]{3,2,1,0:T(8,128)S(1)}, u32[]{:S(2)}, u32[]{:S(2)}) %collective-permute-start.23) | collective-permute-done | bytes 98336 | tf_op jit(solution)/shard_map/ppermute | solution.py:161
  275.7 5.7 %collective-permute-done.24 = f32[6,4,8,128]{3,2,1,0:T(8,128)S(1)} collective-permute-done((f32[6,4,8,128]{3,2,1,0:T(8,128)S(1)}, f32[6,4,8,128]{3,2,1,0:T(8,128)S(1)}, u32[]{:S(2)}, u32[]{:S(2)}) %collective-permute-start.24) | collective-permute-done | bytes 98336 | tf_op jit(solution)/shard_map/ppermute | solution.py:161
  288.2 2.4 collective-permute-done.28
  (113 shorter events, 47.3 us)
Async XLA Ops:
  6.5 204.7 %all-gather.3.cloned.1.call-start = ((), (), s32[]{:S(2)}) async-start(), calls=%async_computation | async-start | bytes 8847360 | tf_op jit(solution)/shard_map/all_gather | solution.py:223
  8.1 19.1 %collective-permute-start.14 = (bf16[6,32,1536]{2,1,0:T(8,128)(2,1)S(1)}, bf16[6,32,1536]{2,1,0:T(8,128)(2,1)S(1)}, u32[]{:S(2)}, u32[]{:S(2)}) collective-permute-start(bf16[6,32,1536]{2,1,0:T(8,128)(2,1)S(1)} %get-tuple-element.33), channel_id=1, source_target_pairs={{6,4},{7,5},{4,2},{5,3},{2,0},{3,1},{14,12},{15,13},{12,10},{13,11... | collective-permute-start | bytes 1769480 | tf_op jit(solution)/shard_map/ppermute | solution.py:184
  9.4 21.8 %collective-permute-start.13 = (bf16[6,32,1536]{2,1,0:T(8,128)(2,1)S(1)}, bf16[6,32,1536]{2,1,0:T(8,128)(2,1)S(1)}, u32[]{:S(2)}, u32[]{:S(2)}) collective-permute-start(bf16[6,32,1536]{2,1,0:T(8,128)(2,1)S(1)} %get-tuple-element.33), channel_id=1, source_target_pairs={{0,2},{1,3},{2,4},{3,5},{4,6},{5,7},{8,10},{9,11},{10,12},{11,13},... | collective-permute-start | bytes 1769480 | tf_op jit(solution)/shard_map/ppermute | solution.py:184
  15.0 26.3 %collective-permute-start.7 = (bf16[6,32,1536]{2,1,0:T(8,128)(2,1)S(1)}, bf16[6,32,1536]{2,1,0:T(8,128)(2,1)S(1)}, u32[]{:S(2)}, u32[]{:S(2)}) collective-permute-start(bf16[6,32,1536]{2,1,0:T(8,128)(2,1)S(1)} %get-tuple-element.34), channel_id=1, source_target_pairs={{0,2},{1,3},{2,4},{3,5},{4,6},{5,7},{8,10},{9,11},{10,12},{11,13},... | collective-permute-start | bytes 1769480 | tf_op jit(solution)/shard_map/ppermute | solution.py:184
  18.9 23.9 %collective-permute-start.8 = (bf16[6,32,1536]{2,1,0:T(8,128)(2,1)S(1)}, bf16[6,32,1536]{2,1,0:T(8,128)(2,1)S(1)}, u32[]{:S(2)}, u32[]{:S(2)}) collective-permute-start(bf16[6,32,1536]{2,1,0:T(8,128)(2,1)S(1)} %get-tuple-element.34), channel_id=1, source_target_pairs={{6,4},{7,5},{4,2},{5,3},{2,0},{3,1},{14,12},{15,13},{12,10},{13,11... | collective-permute-start | bytes 1769480 | tf_op jit(solution)/shard_map/ppermute | solution.py:184
  20.2 32.2 %collective-permute-start.2 = (bf16[6,32,1536]{2,1,0:T(8,128)(2,1)S(1)}, bf16[6,32,1536]{2,1,0:T(8,128)(2,1)S(1)}, u32[]{:S(2)}, u32[]{:S(2)}) collective-permute-start(bf16[6,32,1536]{2,1,0:T(8,128)(2,1)S(1)} %get-tuple-element.35), channel_id=1, source_target_pairs={{6,4},{7,5},{4,2},{5,3},{2,0},{3,1},{14,12},{15,13},{12,10},{13,11... | collective-permute-start | bytes 1769480 | tf_op jit(solution)/shard_map/ppermute | solution.py:184
  27.2 31.4 %collective-permute-start.1 = (bf16[6,32,1536]{2,1,0:T(8,128)(2,1)S(1)}, bf16[6,32,1536]{2,1,0:T(8,128)(2,1)S(1)}, u32[]{:S(2)}, u32[]{:S(2)}) collective-permute-start(bf16[6,32,1536]{2,1,0:T(8,128)(2,1)S(1)} %get-tuple-element.35), channel_id=1, source_target_pairs={{0,2},{1,3},{2,4},{3,5},{4,6},{5,7},{8,10},{9,11},{10,12},{11,13},... | collective-permute-start | bytes 1769480 | tf_op jit(solution)/shard_map/ppermute | solution.py:184
  31.2 34.0 %collective-permute-start.15 = (bf16[6,32,1536]{2,1,0:T(8,128)(2,1)S(1)}, bf16[6,32,1536]{2,1,0:T(8,128)(2,1)}, u32[]{:S(2)}, u32[]{:S(2)}) collective-permute-start(bf16[6,32,1536]{2,1,0:T(8,128)(2,1)S(1)} %collective-permute-done.14), channel_id=1, source_target_pairs={{4,2},{5,3},{2,0},{3,1},{12,10},{13,11},{10,8},{11,9},{20,18},{21,... | collective-permute-start | bytes 1769480 | tf_op jit(solution)/shard_map/ppermute | solution.py:184
  41.3 24.6 %collective-permute-start.17 = (bf16[6,32,1536]{2,1,0:T(8,128)(2,1)S(1)}, bf16[6,32,1536]{2,1,0:T(8,128)(2,1)}, u32[]{:S(2)}, u32[]{:S(2)}) collective-permute-start(bf16[6,32,1536]{2,1,0:T(8,128)(2,1)S(1)} %collective-permute-done.13), channel_id=1, source_target_pairs={{2,4},{3,5},{4,6},{5,7},{10,12},{11,13},{12,14},{13,15},{18,20},{1... | collective-permute-start | bytes 1769480 | tf_op jit(solution)/shard_map/ppermute | solution.py:184
  42.8 25.0 %collective-permute-start.11 = (bf16[6,32,1536]{2,1,0:T(8,128)(2,1)S(1)}, bf16[6,32,1536]{2,1,0:T(8,128)(2,1)}, u32[]{:S(2)}, u32[]{:S(2)}) collective-permute-start(bf16[6,32,1536]{2,1,0:T(8,128)(2,1)S(1)} %collective-permute-done.7), channel_id=1, source_target_pairs={{2,4},{3,5},{4,6},{5,7},{10,12},{11,13},{12,14},{13,15},{18,20},{1... | collective-permute-start | bytes 1769480 | tf_op jit(solution)/shard_map/ppermute | solution.py:184
  53.3 24.5 %collective-permute-start.9 = (bf16[6,32,1536]{2,1,0:T(8,128)(2,1)S(1)}, bf16[6,32,1536]{2,1,0:T(8,128)(2,1)}, u32[]{:S(2)}, u32[]{:S(2)}) collective-permute-start(bf16[6,32,1536]{2,1,0:T(8,128)(2,1)S(1)} %collective-permute-done.8), channel_id=1, source_target_pairs={{4,2},{5,3},{2,0},{3,1},{12,10},{13,11},{10,8},{11,9},{20,18},{21,... | collective-permute-start | bytes 1769480 | tf_op jit(solution)/shard_map/ppermute | solution.py:184
  58.6 31.8 %collective-permute-start.3 = (bf16[6,32,1536]{2,1,0:T(8,128)(2,1)}, bf16[6,32,1536]{2,1,0:T(8,128)(2,1)S(1)}, u32[]{:S(2)}, u32[]{:S(2)}) collective-permute-start(bf16[6,32,1536]{2,1,0:T(8,128)(2,1)} %copy-done.13), channel_id=1, source_target_pairs={{4,2},{5,3},{2,0},{3,1},{12,10},{13,11},{10,8},{11,9},{20,18},{21,... | collective-permute-start | bytes 1769480 | tf_op jit(solution)/shard_map/ppermute | solution.py:184
  65.2 26.5 %collective-permute-start.5 = (bf16[6,32,1536]{2,1,0:T(8,128)(2,1)S(1)}, bf16[6,32,1536]{2,1,0:T(8,128)(2,1)S(1)}, u32[]{:S(2)}, u32[]{:S(2)}) collective-permute-start(bf16[6,32,1536]{2,1,0:T(8,128)(2,1)S(1)} %collective-permute-done.1), channel_id=1, source_target_pairs={{2,4},{3,5},{4,6},{5,7},{10,12},{11,13},{12,14},{13,15},{18,20},{1... | collective-permute-start | bytes 1769480 | tf_op jit(solution)/shard_map/ppermute | solution.py:184
  65.9 26.6 %collective-permute-start.18 = (bf16[6,32,1536]{2,1,0:T(8,128)(2,1)}, bf16[6,32,1536]{2,1,0:T(8,128)(2,1)S(1)}, u32[]{:S(2)}, u32[]{:S(2)}) collective-permute-start(bf16[6,32,1536]{2,1,0:T(8,128)(2,1)} %collective-permute-done.17), channel_id=1, source_target_pairs={{4,6},{5,7},{12,14},{13,15},{20,22},{21,23},{28,30},{29,31}} | collective-permute-start | bytes 1769480 | tf_op jit(solution)/shard_map/ppermute | solution.py:184
  67.8 35.2 %collective-permute-start.16 = (bf16[6,32,1536]{2,1,0:T(8,128)(2,1)}, bf16[6,32,1536]{2,1,0:T(8,128)(2,1)S(1)}, u32[]{:S(2)}, u32[]{:S(2)}) collective-permute-start(bf16[6,32,1536]{2,1,0:T(8,128)(2,1)} %collective-permute-done.15), channel_id=1, source_target_pairs={{2,0},{3,1},{10,8},{11,9},{18,16},{19,17},{26,24},{27,25}} | collective-permute-start | bytes 1769480 | tf_op jit(solution)/shard_map/ppermute | solution.py:184
  77.8 51.4 %collective-permute-start.12 = (bf16[6,32,1536]{2,1,0:T(8,128)(2,1)}, bf16[6,32,1536]{2,1,0:T(8,128)(2,1)S(1)}, u32[]{:S(2)}, u32[]{:S(2)}) collective-permute-start(bf16[6,32,1536]{2,1,0:T(8,128)(2,1)} %collective-permute-done.11), channel_id=1, source_target_pairs={{4,6},{5,7},{12,14},{13,15},{20,22},{21,23},{28,30},{29,31}} | collective-permute-start | bytes 1769480 | tf_op jit(solution)/shard_map/ppermute | solution.py:184
  90.4 39.0 %collective-permute-start.10 = (bf16[6,32,1536]{2,1,0:T(8,128)(2,1)}, bf16[6,32,1536]{2,1,0:T(8,128)(2,1)S(1)}, u32[]{:S(2)}, u32[]{:S(2)}) collective-permute-start(bf16[6,32,1536]{2,1,0:T(8,128)(2,1)} %collective-permute-done.9), channel_id=1, source_target_pairs={{2,0},{3,1},{10,8},{11,9},{18,16},{19,17},{26,24},{27,25}} | collective-permute-start | bytes 1769480 | tf_op jit(solution)/shard_map/ppermute | solution.py:184
  92.5 35.0 %collective-permute-start.4 = (bf16[6,32,1536]{2,1,0:T(8,128)(2,1)S(1)}, bf16[6,32,1536]{2,1,0:T(8,128)(2,1)S(1)}, u32[]{:S(2)}, u32[]{:S(2)}) collective-permute-start(bf16[6,32,1536]{2,1,0:T(8,128)(2,1)S(1)} %collective-permute-done.3), channel_id=1, source_target_pairs={{2,0},{3,1},{10,8},{11,9},{18,16},{19,17},{26,24},{27,25}} | collective-permute-start | bytes 1769480 | tf_op jit(solution)/shard_map/ppermute | solution.py:184
  129.7 120.1 %all-gather.5.cloned.1.call-start = ((), (), s32[]{:S(2)}) async-start(), calls=%async_computation.1 | async-start | bytes 3538944 | tf_op jit(solution)/shard_map/all_gather | solution.py:223
  129.7 6.1 %collective-permute-start = (bf16[6,32,8192]{2,1,0:T(8,128)(2,1)}, bf16[6,32,8192]{2,1,0:T(8,128)(2,1)}, u32[]{:S(2)}, u32[]{:S(2)}) collective-permute-start(bf16[6,32,8192]{2,1,0:T(8,128)(2,1)} %refs_0_.1), channel_id=1, source_target_pairs={{0,1},{1,0},{2,3},{3,2},{4,5},{5,4},{6,7},{7,6},{8,9},{9,8},{10,11... | collective-permute-start | bytes 9437192 | tf_op jit(solution)/shard_map/ppermute | solution.py:187
  131.1 9.7 %collective-permute-start.21 = (bf16[3,6,32,1536]{3,2,1,0:T(8,128)(2,1)}, bf16[3,6,32,1536]{3,2,1,0:T(8,128)(2,1)S(1)}, u32[]{:S(2)}, u32[]{:S(2)}) collective-permute-start(bf16[3,6,32,1536]{3,2,1,0:T(8,128)(2,1)} %pad_maximum_fusion.2.refs_4_), channel_id=1, source_target_pairs={{0,1},{1,0},{2,3},{3,2},{4,5},{5,4},{6,7},{7,6},{8,9},{9,8},{10,11... | collective-permute-start | bytes 5308424 | tf_op jit(solution)/shard_map/ppermute | solution.py:187
  131.5 9.2 %collective-permute-start.20 = (bf16[3,6,32,1536]{3,2,1,0:T(8,128)(2,1)S(1)}, bf16[3,6,32,1536]{3,2,1,0:T(8,128)(2,1)S(1)}, u32[]{:S(2)}, u32[]{:S(2)}) collective-permute-start(bf16[3,6,32,1536]{3,2,1,0:T(8,128)(2,1)S(1)} %pad_maximum_fusion.1.refs_3_), channel_id=1, source_target_pairs={{0,1},{1,0},{2,3},{3,2},{4,5},{5,4},{6,7},{7,6},{8,9},{9,8},{10,11... | collective-permute-start | bytes 5308424 | tf_op jit(solution)/shard_map/ppermute | solution.py:187
  131.6 11.4 %collective-permute-start.19 = (bf16[3,6,32,1536]{3,2,1,0:T(8,128)(2,1)S(1)}, bf16[3,6,32,1536]{3,2,1,0:T(8,128)(2,1)S(1)}, u32[]{:S(2)}, u32[]{:S(2)}) collective-permute-start(bf16[3,6,32,1536]{3,2,1,0:T(8,128)(2,1)S(1)} %pad_maximum_fusion.refs_2_), channel_id=1, source_target_pairs={{0,1},{1,0},{2,3},{3,2},{4,5},{5,4},{6,7},{7,6},{8,9},{9,8},{10,11... | collective-permute-start | bytes 5308424 | tf_op jit(solution)/shard_map/ppermute | solution.py:187
  274.3 7.2 %collective-permute-start.24 = (f32[6,4,8,128]{3,2,1,0:T(8,128)S(1)}, f32[6,4,8,128]{3,2,1,0:T(8,128)S(1)}, u32[]{:S(2)}, u32[]{:S(2)}) collective-permute-start(f32[6,4,8,128]{3,2,1,0:T(8,128)S(1)} %fusion.2), channel_id=1, source_target_pairs={{0,4},{1,5},{2,6},{3,7},{4,0},{5,1},{6,2},{7,3},{8,12},{9,13},{10,... | collective-permute-start | bytes 294920 | tf_op jit(solution)/shard_map/ppermute | solution.py:161
  (26 other events, 255.1 us)
Sparse Core Ops, SparseCore 0:
  129.8 81.4 all-gather.2
  212.9 36.8 all-gather.4
